TPU v7x, 32 devices: a whole 2x2x4 slice. The times are simulated.
32 devices in a mesh: ex: 8 (over z, x), tp: 4 (over y, core).
Axes of the slice: x: 2, y: 2, z: 4, core: 2. Of those that a mesh axis runs over, the one named last changes fastest.
Arguments:
- inputs: bfloat16 [1024, 768], P('ex'), may hold values from -6 to 6
- routes: int32 [1024, 2], P('ex'), may hold values from 0 to 7, all different within a row; in each aligned block of 128 rows (0 to 127, 128 to 255, ...) at most 64 rows name the same one
- lengths: int32 [8, 4], P('ex'), may hold values from 1 to 96, 128 in all within a row
- w_query: bfloat16 [768, 768], P(None, 'tp'), may hold values from -0.21875 to 0.21875
- w_key: bfloat16 [768, 768], P(None, 'tp'), may hold values from -0.21875 to 0.21875
- w_value: bfloat16 [768, 768], P(None, 'tp'), may hold values from -0.21875 to 0.21875
- w_attn_out: bfloat16 [768, 768], P('tp'), may hold values from -0.875 to 0.875
- gain_attn: float32 [768], replicated, may hold values from 0.25 to 1.75
- gain_moe: float32 [768], replicated, may hold values from 0.25 to 1.75
- rel_bias: float32 [32, 12], P(None, 'tp'), may hold values from -4 to 4
- w_router: bfloat16 [768, 8], replicated, may hold values from -0.15625 to 0.15625
- w_in: bfloat16 [8, 768, 3072], P('ex', None, 'tp'), may hold values from -0.21875 to 0.21875
- w_out: bfloat16 [8, 3072, 768], P('ex', 'tp'), may hold values from -0.109375 to 0.109375
- cotangent: bfloat16 [1024, 768], P('ex'), may hold values from -6 to 6
Outputs:
- output: bfloat16 [1024, 768], P('ex')
- grad_inputs: bfloat16 [1024, 768], P('ex')
- grad_w_query: float32 [768, 768], P(None, 'tp')
- grad_w_key: float32 [768, 768], P(None, 'tp')
- grad_w_value: float32 [768, 768], P(None, 'tp')
- grad_w_attn_out: float32 [768, 768], P('tp')
- grad_gain_attn: float32 [768], replicated
- grad_gain_moe: float32 [768], replicated
- grad_rel_bias: float32 [32, 12], P(None, 'tp')
- grad_w_router: float32 [768, 8], replicated
- grad_w_in: float32 [8, 768, 3072], P('ex', None, 'tp')
- grad_w_out: float32 [8, 3072, 768], P('ex', 'tp')
Inputs may be any that keep to these rules, and one draw needn't show every extreme that they name: `routes`: each row names two different experts. The rows of one index of ex name any one expert at most 64 times, a bound that some block reaches. `lengths`: each row sums to 128 and its largest entry is exactly 96.
All inputs are finite; a program needn't handle non-finite values.
Results may differ from a plain program's by a relative error of at most 0.017.
Values may be sent and summed in bfloat16 or wider, within the bound.
A program may use at most 128 MiB of HBM per device.

v0:
```python
from functools import partial
import math
import jax
import jax.numpy as jnp
from jax import lax
from jax.sharding import PartitionSpec as P

eps = 1e-06
highest = lax.Precision.HIGHEST
bucket_edges = [math.ceil(16 * 8 ** (number / 16)) for number in range(1, 16)]


def rms_scale(values):
    return lax.rsqrt(jnp.mean(values * values, -1, keepdims=True) + eps)


def bucket_of(length):
    positions = jnp.arange(length, dtype=jnp.int32)
    offsets = positions[:, None] - positions[None, :]
    distance = jnp.maximum(offsets, 0)
    counted = jnp.zeros_like(distance)
    for border in bucket_edges:
        counted = counted + (distance >= border).astype(jnp.int32)
    return jnp.where(distance < 16, distance, 16 + counted)


def contract_rows(left_side, right_side):
    return lax.dot_general(
        left_side, right_side, (((0,), (0,)), ((), ())), preferred_element_type=jnp.float32
    )


def contract_cols(left_side, right_side):
    return lax.dot_general(
        left_side, right_side, (((1,), (1,)), ((), ())), preferred_element_type=jnp.float32
    )


def shards(
    inputs,
    routes,
    lengths,
    w_query,
    w_key,
    w_value,
    w_attn_out,
    gain_attn,
    gain_moe,
    rel_bias,
    w_router,
    w_in,
    w_out,
    cotangent,
):
    tok_rows, model_width = inputs.shape
    local_heads = rel_bias.shape[1]
    head_dim = w_query.shape[1] // local_heads
    attn_scale = head_dim ** (-0.5)
    experts = w_router.shape[1]
    ex_devices = lax.axis_size("ex")
    local_experts = w_in.shape[0]
    capacity = 4 * tok_rows // experts
    pair_count = 2 * tok_rows
    inputs_f = inputs.astype(jnp.float32)
    scale_a = rms_scale(inputs_f)
    normed_a = inputs_f * scale_a
    attn_in = (normed_a * gain_attn).astype(jnp.bfloat16)
    query_b = (
        jnp.dot(attn_in, w_query, preferred_element_type=jnp.float32)
        .astype(jnp.bfloat16)
        .reshape(tok_rows, local_heads, head_dim)
    )
    key_b = (
        jnp.dot(attn_in, w_key, preferred_element_type=jnp.float32)
        .astype(jnp.bfloat16)
        .reshape(tok_rows, local_heads, head_dim)
    )
    value_b = (
        jnp.dot(attn_in, w_value, preferred_element_type=jnp.float32)
        .astype(jnp.bfloat16)
        .reshape(tok_rows, local_heads, head_dim)
    )
    buckets = bucket_of(tok_rows)
    one_hot = (
        buckets[None] == jnp.arange(rel_bias.shape[0], dtype=jnp.int32)[:, None, None]
    ).astype(jnp.float32)
    bias_full = jnp.einsum("bij,bh->hij", one_hot, rel_bias, precision=highest)
    seq_ends = jnp.cumsum(lengths[0])
    positions = jnp.arange(tok_rows, dtype=jnp.int32)
    segments = jnp.sum((positions[:, None] >= seq_ends[None, :]).astype(jnp.int32), -1)
    allowed = (segments[:, None] == segments[None, :]) & (positions[:, None] >= positions[None, :])

    def score_of(queries_in, keys_in):
        raw_scores = (
            jnp.einsum("ihd,jhd->hij", queries_in, keys_in, preferred_element_type=jnp.float32)
            * attn_scale
        )
        return jnp.where(allowed[None], raw_scores + bias_full, -1e30)

    scores = score_of(query_b, key_b)
    row_max = jnp.max(scores, -1, keepdims=True)
    log_sum = row_max + jnp.log(jnp.sum(jnp.exp(scores - row_max), -1, keepdims=True))
    probabilities = jnp.exp(scores - log_sum)
    probs_low = probabilities.astype(jnp.bfloat16)
    mixed_heads = (
        jnp.einsum("hij,jhd->ihd", probs_low, value_b, preferred_element_type=jnp.float32)
        .astype(jnp.bfloat16)
        .reshape(tok_rows, -1)
    )
    head_part = jnp.dot(mixed_heads, w_attn_out, preferred_element_type=jnp.float32)
    residual = inputs_f + lax.psum(head_part, "tp")
    scale_m = rms_scale(residual)
    normed_m = residual * scale_m
    moe_in = (normed_m * gain_moe).astype(jnp.bfloat16)
    logits = jnp.dot(moe_in, w_router, preferred_element_type=jnp.float32)
    expert_ids = jnp.arange(experts, dtype=jnp.int32)
    route_hot = (routes[:, :, None] == expert_ids[None, None, :]).astype(jnp.float32)
    chosen_logits = jnp.sum(route_hot * logits[:, None, :], -1)
    gate_max = jnp.max(chosen_logits, -1, keepdims=True)
    gate_exp = jnp.exp(chosen_logits - gate_max)
    gate_values = gate_exp / jnp.sum(gate_exp, -1, keepdims=True)
    pair_routes = routes.reshape(-1)
    pair_hot = (pair_routes[:, None] == expert_ids[None, :]).astype(jnp.int32)
    slot_index = jnp.sum(pair_hot * jnp.cumsum(pair_hot, 0), -1) - 1
    pair_slots = pair_routes * capacity + slot_index
    members = (
        jnp.full((experts * capacity,), pair_count, jnp.int32)
        .at[pair_slots]
        .set(jnp.arange(pair_count, dtype=jnp.int32))
    )
    padded = jnp.concatenate([moe_in, jnp.zeros((1, model_width), jnp.bfloat16)], 0)
    send_rows = padded[members // 2].reshape(experts, capacity, model_width)
    arrived = lax.all_to_all(send_rows, "ex", split_axis=0, concat_axis=0, tiled=True)
    slot_count = arrived.shape[1]
    grouped = arrived.reshape(ex_devices, local_experts, slot_count, model_width)
    pre_act = jnp.einsum("slcd,ldf->slcf", grouped, w_in, preferred_element_type=jnp.float32)
    act_low = jax.nn.gelu(pre_act, approximate=True).astype(jnp.bfloat16)
    partial_out = jnp.einsum("slcf,lfd->slcd", act_low, w_out, preferred_element_type=jnp.float32)
    partial_out = partial_out.reshape(ex_devices * local_experts, slot_count, model_width)
    owned_rows = lax.psum_scatter(
        partial_out.astype(jnp.bfloat16), "tp", scatter_dimension=2, tiled=True
    )
    returned = lax.all_to_all(owned_rows, "ex", split_axis=0, concat_axis=0, tiled=True)
    returned, kept_rows, kept_pre = (
        returned,
        arrived,
        pre_act.reshape(ex_devices * local_experts, slot_count, -1),
    )
    expert_out = lax.all_gather(returned, "tp", axis=2, tiled=True).reshape(
        experts * capacity, model_width
    )
    pair_out = expert_out[pair_slots].reshape(tok_rows, 2, model_width).astype(jnp.float32)
    result = residual + jnp.sum(gate_values[:, :, None] * pair_out, 1)
    output = result.astype(jnp.bfloat16)
    grad_out = cotangent.astype(jnp.float32)
    gate_grad = jnp.sum(grad_out[:, None, :] * pair_out, -1)
    logit_pair = gate_values * (gate_grad - jnp.sum(gate_values * gate_grad, -1, keepdims=True))
    logit_grads = jnp.sum(logit_pair[:, :, None] * route_hot, 1)
    grad_router = jnp.dot(moe_in.astype(jnp.float32).T, logit_grads, precision=highest)
    moe_grad = jnp.dot(logit_grads, w_router.astype(jnp.float32).T, precision=highest)
    pair_grads = (
        (gate_values[:, :, None] * grad_out[:, None, :])
        .astype(jnp.bfloat16)
        .reshape(pair_count, model_width)
    )
    padded_grads = jnp.concatenate([pair_grads, jnp.zeros((1, model_width), jnp.bfloat16)], 0)
    send_grad_rows = padded_grads[members].reshape(experts, capacity, model_width)
    arrived_grads = lax.all_to_all(send_grad_rows, "ex", split_axis=0, concat_axis=0, tiled=True)
    grad_group = arrived_grads.reshape(ex_devices, local_experts, capacity, model_width)
    act_grad = jnp.einsum("slcd,lfd->slcf", grad_group, w_out, preferred_element_type=jnp.float32)
    pre_keep = kept_pre.reshape(ex_devices, local_experts, capacity, -1)
    act_value, gelu_back = jax.vjp(partial(jax.nn.gelu, approximate=True), pre_keep)
    pre_grad = gelu_back(act_grad)[0].astype(jnp.bfloat16)
    act_low = act_value.astype(jnp.bfloat16)
    grad_w_out = jnp.einsum(
        "slcf,slcd->lfd", act_low, grad_group, preferred_element_type=jnp.float32
    )
    rows_group = kept_rows.reshape(ex_devices, local_experts, capacity, model_width)
    grad_w_in = jnp.einsum(
        "slcd,slcf->ldf", rows_group, pre_grad, preferred_element_type=jnp.float32
    )
    row_part = jnp.einsum("slcf,ldf->slcd", pre_grad, w_in, preferred_element_type=jnp.float32)
    row_part = row_part.reshape(ex_devices * local_experts, capacity, model_width)
    row_share = lax.psum_scatter(row_part, "tp", scatter_dimension=2, tiled=True).astype(
        jnp.bfloat16
    )
    row_back = lax.all_to_all(row_share, "ex", split_axis=0, concat_axis=0, tiled=True)
    row_full = lax.all_gather(row_back, "tp", axis=2, tiled=True).reshape(
        experts * capacity, model_width
    )
    moe_grad = moe_grad + jnp.sum(
        row_full[pair_slots].reshape(tok_rows, 2, model_width).astype(jnp.float32), 1
    )
    grad_gain_moe = jnp.sum(moe_grad * normed_m, 0)
    normed_grad_m = moe_grad * gain_moe
    resid_grad = grad_out + scale_m * (
        normed_grad_m - normed_m * jnp.mean(normed_grad_m * normed_m, -1, keepdims=True)
    )
    attn_grad = resid_grad.astype(jnp.bfloat16)
    grad_w_attn_out = contract_rows(mixed_heads, attn_grad)
    mixed_grad = (
        contract_cols(attn_grad, w_attn_out)
        .astype(jnp.bfloat16)
        .reshape(tok_rows, local_heads, head_dim)
    )
    scores_again = score_of(query_b, key_b)
    probs_again = jnp.exp(scores_again - log_sum)
    prob_grad = jnp.einsum("ihd,jhd->hij", mixed_grad, value_b, preferred_element_type=jnp.float32)
    value_grad = jnp.einsum(
        "hij,ihd->jhd",
        probs_again.astype(jnp.bfloat16),
        mixed_grad,
        preferred_element_type=jnp.float32,
    ).astype(jnp.bfloat16)
    score_grad = probs_again * (prob_grad - jnp.sum(probs_again * prob_grad, -1, keepdims=True))
    grad_rel_bias = jnp.einsum("hij,bij->bh", score_grad, one_hot, precision=highest)
    score_low = score_grad.astype(jnp.bfloat16)
    query_grad = (
        (
            jnp.einsum("hij,jhd->ihd", score_low, key_b, preferred_element_type=jnp.float32)
            * attn_scale
        )
        .astype(jnp.bfloat16)
        .reshape(tok_rows, -1)
    )
    key_grad = (
        (
            jnp.einsum("hij,ihd->jhd", score_low, query_b, preferred_element_type=jnp.float32)
            * attn_scale
        )
        .astype(jnp.bfloat16)
        .reshape(tok_rows, -1)
    )
    value_flat = value_grad.reshape(tok_rows, -1)
    grad_w_query = contract_rows(attn_in, query_grad)
    grad_w_key = contract_rows(attn_in, key_grad)
    grad_w_value = contract_rows(attn_in, value_flat)
    input_part = (
        contract_cols(query_grad, w_query)
        + contract_cols(key_grad, w_key)
        + contract_cols(value_flat, w_value)
    )
    input_grad = lax.psum(input_part.astype(jnp.bfloat16), "tp").astype(jnp.float32)
    grad_gain_attn = jnp.sum(input_grad * normed_a, 0)
    normed_grad_a = input_grad * gain_attn
    grad_inputs = (
        resid_grad
        + scale_a
        * (normed_grad_a - normed_a * jnp.mean(normed_grad_a * normed_a, -1, keepdims=True))
    ).astype(jnp.bfloat16)
    dense_sums = lax.psum(
        (
            grad_w_query,
            grad_w_key,
            grad_w_value,
            grad_w_attn_out,
            grad_gain_attn,
            grad_gain_moe,
            grad_rel_bias,
            grad_router,
        ),
        "ex",
    )
    return (
        output,
        grad_inputs,
        dense_sums[0],
        dense_sums[1],
        dense_sums[2],
        dense_sums[3],
        dense_sums[4],
        dense_sums[5],
        dense_sums[6],
        dense_sums[7],
        grad_w_in,
        grad_w_out,
    )


def solution(mesh):
    placed = (
        P("ex", None),
        P("ex", None),
        P("ex", None),
        P(None, "tp"),
        P(None, "tp"),
        P(None, "tp"),
        P("tp", None),
        P(),
        P(),
        P(None, "tp"),
        P(),
        P("ex", None, "tp"),
        P("ex", "tp", None),
        P("ex", None),
    )
    return jax.shard_map(
        shards,
        mesh=mesh,
        in_specs=placed,
        out_specs=(
            P("ex", None),
            P("ex", None),
            P(None, "tp"),
            P(None, "tp"),
            P(None, "tp"),
            P("tp", None),
            P(),
            P(),
            P(None, "tp"),
            P(),
            P("ex", None, "tp"),
            P("ex", "tp", None),
        ),
        check_vma=False,
    )
```

profile of v0, /device:TPU:0, one launch (start us, length us, event | category | flops | bytes accessed | tf_op | source)
XLA Modules:
  0.0 362.4 jit_solution(3472108545965280200)
XLA Ops:
  18.6 31.8 %all-reduce.8.cloned.1.call-done = f32[128,768]{1,0:T(8,128)} async-done(((f32[128,768]{1,0:T(8,128)}), f32[128,768]{1,0:T(8,128)}) %all-reduce.8.cloned.1.call-update) | async-done | bytes 393232 | tf_op jit(solution)/shard_map/psum | solution.py:111
  52.9 2.7 gather_fusion
  55.6 5.6 %all-to-all-start = ((bf16[8,64,768]{2,1,0:T(8,128)(2,1)}), bf16[8,64,768]{2,1,0:T(8,128)(2,1)}, u32[]{:S(2)}, u32[]{:S(2)}) async-start(bf16[8,64,768]{2,1,0:T(8,128)(2,1)} %bitcast.13), calls=%async_computation | async-start | bytes 1572864 | tf_op jit(solution)/shard_map/all_to_all | solution.py:133
  65.4 2.7 gather_fusion.2
  68.1 12.4 %all-to-all-done = bf16[8,64,768]{2,1,0:T(8,128)(2,1)} async-done(((bf16[8,64,768]{2,1,0:T(8,128)(2,1)}), bf16[8,64,768]{2,1,0:T(8,128)(2,1)}, u32[]{:S(2)}, u32[]{:S(2)}) %all-to-all-start) | async-done | bytes 786464 | tf_op jit(solution)/shard_map/all_to_all | solution.py:133
  80.5 4.3 %all-to-all-start.2 = ((bf16[8,64,768]{2,1,0:T(8,128)(2,1)}), bf16[8,64,768]{2,1,0:T(8,128)(2,1)}, u32[]{:S(2)}, u32[]{:S(2)}) async-start(bf16[8,64,768]{2,1,0:T(8,128)(2,1)} %bitcast.25), calls=%async_computation.2 | async-start | bytes 1572864 | tf_op jit(solution)/shard_map/all_to_all | solution.py:168
  93.9 10.5 %all-to-all-done.2 = bf16[8,64,768]{2,1,0:T(8,128)(2,1)} async-done(((bf16[8,64,768]{2,1,0:T(8,128)(2,1)}), bf16[8,64,768]{2,1,0:T(8,128)(2,1)}, u32[]{:S(2)}, u32[]{:S(2)}) %all-to-all-start.2) | async-done | bytes 786464 | tf_op jit(solution)/shard_map/all_to_all | solution.py:168
  104.4 3.1 fusion.13
  108.4 2.1 fusion.16
  110.5 2.3 copy.98
  112.7 3.7 %reshape.492 = f32[768,512]{1,0:T(8,128)} reshape(f32[768,8,64]{2,1,0:T(8,128)} %bitcast.149) | data formatting | bytes 3145728
  120.1 5.5 %all-to-all-start.1 = ((bf16[8,64,192]{2,1,0:T(8,128)(2,1)}), bf16[8,64,192]{2,1,0:T(8,128)(2,1)S(1)}, u32[]{:S(2)}, u32[]{:S(2)}) async-start(bf16[8,64,192]{2,1,0:T(8,128)(2,1)} %copy.97), calls=%async_computation.1 | async-start | bytes 524288 | tf_op jit(solution)/shard_map/all_to_all | solution.py:143
  126.4 8.1 %all-to-all-done.1 = bf16[8,64,192]{2,1,0:T(8,128)(2,1)S(1)} async-done(((bf16[8,64,192]{2,1,0:T(8,128)(2,1)}), bf16[8,64,192]{2,1,0:T(8,128)(2,1)S(1)}, u32[]{:S(2)}, u32[]{:S(2)}) %all-to-all-start.1) | async-done | bytes 196640 | tf_op jit(solution)/shard_map/all_to_all | solution.py:143
  134.8 20.2 %all_gather.6 = bf16[8,64,768]{1,0,2:T(8,128)(2,1)} all-gather(bf16[8,64,192]{1,0,2:T(8,128)(2,1)S(1)} %copy.81), channel_id=1, replica_groups=mesh['ex'=8,'tp'=4] {'tp'}, dimensions={2}, use_global_device_ids=true | all-gather | bytes 983040 | tf_op jit(solution)/shard_map/all_gather | solution.py:149
  158.6 2.4 multiply_reduce_fusion
  163.3 3.4 all-to-all-start.3
  166.8 9.5 %all-to-all-done.3 = bf16[8,64,192]{2,1,0:T(8,128)(2,1)S(1)} async-done(((bf16[8,64,192]{2,1,0:T(8,128)(2,1)}), bf16[8,64,192]{2,1,0:T(8,128)(2,1)S(1)}, u32[]{:S(2)}, u32[]{:S(2)}) %all-to-all-start.3) | async-done | bytes 196640 | tf_op jit(solution)/shard_map/all_to_all | solution.py:187
  176.6 13.6 %all_gather.7 = bf16[8,64,768]{1,0,2:T(8,128)(2,1)} all-gather(bf16[8,64,192]{1,0,2:T(8,128)(2,1)S(1)} %copy.86), channel_id=1, replica_groups=mesh['ex'=8,'tp'=4] {'tp'}, dimensions={2}, use_global_device_ids=true | all-gather | bytes 983040 | tf_op jit(solution)/shard_map/all_gather | solution.py:188
  206.7 3.5 convolution_bitcast_fusion.1
  210.2 3.5 convolution_bitcast_fusion
  215.2 21.0 %all-reduce.10.cloned.1.call-done = bf16[128,768]{1,0:T(8,128)(2,1)} async-done(((bf16[128,768]{1,0:T(8,128)(2,1)}), bf16[128,768]{1,0:T(8,128)(2,1)}) %all-reduce.10.cloned.1.call-update) | async-done | bytes 196624 | tf_op jit(solution)/shard_map/psum | solution.py:243
  237.4 40.3 %all-reduce.2 = (f32[768]{0:T(1024)}, f32[768]{0:T(1024)}, f32[32,3]{0,1:T(4,128)}, f32[768,8]{0,1:T(8,128)}) all-reduce(f32[768]{0:T(1024)S(1)} %get-tuple-element.16, f32[768]{0:T(1024)S(1)} %get-tuple-element.12, f32[32,3]{0,1:T(4,128)S(1)} %fusion.25, f32[768,8]{0,1:T(8,128)S(1)} %fusion.98), channel_id=1, replica_groups=mesh['ex'=8,'tp'=4] {'ex'}, use_global_device_ids=true, to_apply=%region_30.31 | all-reduce | flops 7776 | bytes 62208 | tf_op jit(solution)/shard_map/psum | solution.py:251
  279.4 71.9 %all-reduce.12.cloned.1.call-done = (f32[768,192]{0,1:T(8,128)}, f32[768,192]{0,1:T(8,128)}, f32[768,192]{0,1:T(8,128)}, f32[192,768]{1,0:T(8,128)}) async-done(((f32[768,192]{0,1:T(8,128)}, f32[768,192]{0,1:T(8,128)}, f32[768,192]{0,1:T(8,128)}, f32[192,768]{1,0:T(8,128)}), (f32[768,192]{0,1:T(8,128)}, f32[768,192]{0,1:T(8,128)}, f32[768,192]{0,1:T(8,128)}, ...) | async-done | bytes 2359312 | tf_op jit(solution)/shard_map/psum | solution.py:251
  351.4 2.0 copy.106
  (209 shorter events, 61.5 us)
Async XLA Ops:
  7.2 80.8 %copy-start = (bf16[1,768,768]{2,1,0:T(8,128)(2,1)S(1)}, bf16[1,768,768]{2,1,0:T(8,128)(2,1)}, u32[]{:S(2)}) copy-start(bf16[1,768,768]{2,1,0:T(8,128)(2,1)} %param.26) | copy-start | bytes 3538948
  7.2 4.5 %copy-start.1 = (bf16[128,768]{1,0:T(8,128)(2,1)S(1)}, bf16[128,768]{1,0:T(8,128)(2,1)}, u32[]{:S(2)}) copy-start(bf16[128,768]{1,0:T(8,128)(2,1)} %param.14) | copy-start | bytes 589828
  7.2 4.5 %copy-start.26 = (f32[768]{0:T(1024)S(1)}, f32[768]{0:T(1024)}, u32[]{:S(2)}) copy-start(f32[768]{0:T(1024)} %param.21) | copy-start | bytes 9220
  7.2 4.5 %copy-start.16 = (bf16[768,192]{0,1:T(8,128)(2,1)S(1)}, bf16[768,192]{0,1:T(8,128)(2,1)}, u32[]{:S(2)}) copy-start(bf16[768,192]{0,1:T(8,128)(2,1)} %param.17) | copy-start | bytes 884740
  7.2 4.8 %copy-start.18 = (bf16[768,192]{0,1:T(8,128)(2,1)S(1)}, bf16[768,192]{0,1:T(8,128)(2,1)}, u32[]{:S(2)}) copy-start(bf16[768,192]{0,1:T(8,128)(2,1)} %param.18) | copy-start | bytes 884740
  7.2 5.1 %copy-start.45 = (s32[1,4]{1,0:T(1,128)S(1)}, s32[1,4]{1,0:T(1,128)}, u32[]{:S(2)}) copy-start(s32[1,4]{1,0:T(1,128)} %param.16) | copy-start | bytes 52
  7.3 43.1 %all-reduce.8.cloned.1.call-start = ((), (), s32[]{:S(2)}) async-start(), calls=%async_computation.6 | async-start | bytes 786432 | tf_op jit(solution)/shard_map/psum | solution.py:111
  7.4 5.3 %copy-start.27 = (s32[128,128]{1,0:T(8,128)}, s32[128,128]{1,0:T(8,128)S(1)}, u32[]{:S(2)}) copy-start(s32[128,128]{1,0:T(8,128)S(1)} %compare_select_fusion) | copy-start | bytes 196612
  12.4 39.1 %copy-start.22 = (bf16[128,192]{0,1:T(8,128)(2,1)}, bf16[128,192]{0,1:T(8,128)(2,1)S(1)}, u32[]{:S(2)}) copy-start(bf16[128,192]{0,1:T(8,128)(2,1)S(1)} %convolution_convert_fusion.4) | copy-start | bytes 147460
  13.0 39.0 %copy-start.30 = (f32[768]{0:T(1024)S(1)}, f32[768]{0:T(1024)}, u32[]{:S(2)}) copy-start(f32[768]{0:T(1024)} %param.22) | copy-start | bytes 9220
  55.6 5.6 %copy-start.4 = (bf16[128,768]{1,0:T(8,128)(2,1)S(1)}, bf16[128,768]{1,0:T(8,128)(2,1)}, u32[]{:S(2)}) copy-start(bf16[128,768]{1,0:T(8,128)(2,1)} %param.27) | copy-start | bytes 589828
  55.6 24.9 %all-to-all-start = ((bf16[8,64,768]{2,1,0:T(8,128)(2,1)}), bf16[8,64,768]{2,1,0:T(8,128)(2,1)}, u32[]{:S(2)}, u32[]{:S(2)}) async-start(bf16[8,64,768]{2,1,0:T(8,128)(2,1)} %bitcast.13), calls=%async_computation | async-start | bytes 1572864 | tf_op jit(solution)/shard_map/all_to_all | solution.py:133
  80.5 23.9 %all-to-all-start.2 = ((bf16[8,64,768]{2,1,0:T(8,128)(2,1)}), bf16[8,64,768]{2,1,0:T(8,128)(2,1)}, u32[]{:S(2)}, u32[]{:S(2)}) async-start(bf16[8,64,768]{2,1,0:T(8,128)(2,1)} %bitcast.25), calls=%async_computation.2 | async-start | bytes 1572864 | tf_op jit(solution)/shard_map/all_to_all | solution.py:168
  84.8 33.1 %reduce-scatter.7.cloned.1.call-start = ((), (), s32[]{:S(2)}) async-start(), calls=%async_computation.8 | async-start | bytes 983040
  93.6 67.4 %reduce-scatter.9.cloned.1.call-start = ((), (), s32[]{:S(2)}) async-start(), calls=%async_computation.9 | async-start | bytes 1966080
  116.5 9.1 %copy-start.5 = (bf16[128,768]{1,0:T(8,128)(2,1)S(1)}, bf16[128,768]{1,0:T(8,128)(2,1)}, u32[]{:S(2)}) copy-start(bf16[128,768]{1,0:T(8,128)(2,1)} %param.27) | copy-start | bytes 589828
  116.5 9.9 %copy-start.43 = (s32[256,1]{0,1:T(1,128)S(1)}, s32[256,1]{0,1:T(1,128)}, u32[]{:S(2)}) copy-start(s32[256,1]{0,1:T(1,128)} %copy-done.42) | copy-start | bytes 3076
  120.1 14.4 %all-to-all-start.1 = ((bf16[8,64,192]{2,1,0:T(8,128)(2,1)}), bf16[8,64,192]{2,1,0:T(8,128)(2,1)S(1)}, u32[]{:S(2)}, u32[]{:S(2)}) async-start(bf16[8,64,192]{2,1,0:T(8,128)(2,1)} %copy.97), calls=%async_computation.1 | async-start | bytes 524288 | tf_op jit(solution)/shard_map/all_to_all | solution.py:143
  158.6 8.2 %copy-start.34 = (f32[128]{0:T(128)S(1)}, f32[128]{0:T(128)}, u32[]{:S(2)}) copy-start(f32[128]{0:T(128)} %copy-done.33) | copy-start | bytes 1540
  158.6 8.2 %copy-start.39 = (f32[128]{0:T(128)S(1)}, f32[128]{0:T(128)}, u32[]{:S(2)}) copy-start(f32[128]{0:T(128)} %copy-done.38) | copy-start | bytes 1540
  158.6 8.2 %copy-start.32 = (s32[128,2]{0,1:T(2,128)S(1)}, s32[128,2]{0,1:T(2,128)}, u32[]{:S(2)}) copy-start(s32[128,2]{0,1:T(2,128)} %param.15) | copy-start | bytes 3076
  163.3 13.1 %all-to-all-start.3 = ((bf16[8,64,192]{2,1,0:T(8,128)(2,1)}), bf16[8,64,192]{2,1,0:T(8,128)(2,1)S(1)}, u32[]{:S(2)}, u32[]{:S(2)}) async-start(bf16[8,64,192]{2,1,0:T(8,128)(2,1)} %copy.99), calls=%async_computation.3 | async-start | bytes 524288 | tf_op jit(solution)/shard_map/all_to_all | solution.py:187
  166.7 69.5 %all-reduce.10.cloned.1.call-start = ((), (), s32[]{:S(2)}) async-start(), calls=%async_computation.7 | async-start | bytes 393216 | tf_op jit(solution)/shard_map/psum | solution.py:243
  205.5 145.8 %all-reduce.12.cloned.1.call-start = ((), (), s32[]{:S(2)}) async-start(), calls=%async_computation.10 | async-start | bytes 4718592 | tf_op jit(solution)/shard_map/psum | solution.py:251
  (35 other events, 81.6 us)
Sparse Core Ops, SparseCore 0:
  15.0 35.3 all-reduce.7
  93.7 24.1 reduce-scatter.6
  121.0 34.1 reduce-scatter.8
  205.6 30.5 all-reduce.9
  240.5 110.7 all-reduce.11
where the time goes:
time: 364 us; the launch traced here: 362 us
  waiting for transfers between devices  167 us (46%)
  blocking collectives  74 us (20%)
  local copies, waits for them, and re-layouts  42.2 us (12%)
  matrix products  31.6 us (9%)
  starting transfers between devices  19.3 us (5%)
  between operations  14.6 us (4%)
  other arithmetic  14 us (4%)
    psum x1, waiting for transfers between devices, shards(): lax.psum((grad_w_query, grad_w_key, grad_w_value, grad_w_attn_out, grad_g...  71.9 us
    psum x1, blocking collectives, shards(): lax.psum((grad_w_query, grad_w_key, grad_w_value, grad_w_attn_out, grad_g...  40.3 us
    psum x1, waiting for transfers between devices, shards(): residual = inputs_f + lax.psum(head_part, 'tp')  31.8 us
    unnamed x113, local copies, waits for them, and re-layouts  23.8 us
    psum x1, waiting for transfers between devices, shards(): lax.psum(input_part.astype(jnp.bfloat16), 'tp').astype(jnp.float32)  21 us
    all_gather x1, blocking collectives, shards(): lax.all_gather(returned, 'tp', axis=2, tiled=True)  20.2 us
    all_gather x1, blocking collectives, shards(): lax.all_gather(row_back, 'tp', axis=2, tiled=True)  13.6 us
    all_to_all x1, waiting for transfers between devices, shards(): lax.all_to_all(send_rows, 'ex', split_axis=0, concat_axis=0, tiled=True)  12.4 us
  transfers between devices with their start and end apart: 9, of which 8 were waited for; matrix products, arithmetic and copies ran while one was open for 14% of the time, Pallas kernels for 0%

commit v1 on v0

--- a/solution.py
+++ b/solution.py
@@ -1,3 +1,4 @@
+import functools
 from functools import partial
 import math
 import jax
@@ -8,6 +9,13 @@
 eps = 1e-06
 highest = lax.Precision.HIGHEST
 bucket_edges = [math.ceil(16 * 8 ** (number / 16)) for number in range(1, 16)]
+
+
+def _place_cells(body, axis_id):
+    return jnp.sum(lax.all_gather(body, axis_name=axis_id), 0)
+
+
+flows_launch = functools.partial(_place_cells, axis_id="tp")
 
 
 def rms_scale(values):
@@ -108,7 +116,7 @@
         .reshape(tok_rows, -1)
     )
     head_part = jnp.dot(mixed_heads, w_attn_out, preferred_element_type=jnp.float32)
-    residual = inputs_f + lax.psum(head_part, "tp")
+    residual = inputs_f + flows_launch(head_part)
     scale_m = rms_scale(residual)
     normed_m = residual * scale_m
     moe_in = (normed_m * gain_moe).astype(jnp.bfloat16)

time: 364 us -> 352 us (0.967)
  waiting for transfers between devices: 167 us -> 155 us
    psum x1 -> x0, waiting for transfers between devices: 31.8 us -> none  [shards(): residual = inputs_f + lax.psum(head_part, 'tp')]
    all_gather x0 -> x1, waiting for transfers between devices: none -> 18.8 us  [_place_cells(): return jnp.sum(lax.all_gather(body, axis_name=axis_id), 0)]
where the time goes in v1:
time: 352 us; the launch traced here: 351 us
  waiting for transfers between devices  155 us (44%)
  blocking collectives  73.7 us (21%)
  local copies, waits for them, and re-layouts  42.2 us (12%)
  matrix products  31.5 us (9%)
  starting transfers between devices  19.3 us (5%)
  other arithmetic  14.6 us (4%)
  between operations  14.6 us (4%)
    psum x1, waiting for transfers between devices, shards(): lax.psum((grad_w_query, grad_w_key, grad_w_value, grad_w_attn_out, grad_g...  72.7 us
    psum x1, blocking collectives, shards(): lax.psum((grad_w_query, grad_w_key, grad_w_value, grad_w_attn_out, grad_g...  40.1 us
    unnamed x113, local copies, waits for them, and re-layouts  23.8 us
    psum x1, waiting for transfers between devices, shards(): lax.psum(input_part.astype(jnp.bfloat16), 'tp').astype(jnp.float32)  21 us
    all_gather x1, blocking collectives, shards(): lax.all_gather(returned, 'tp', axis=2, tiled=True)  20 us
    all_gather x1, waiting for transfers between devices, _place_cells(): return jnp.sum(lax.all_gather(body, axis_name=axis_id), 0)  18.8 us
    all_to_all x1, waiting for transfers between devices, shards(): lax.all_to_all(send_rows, 'ex', split_axis=0, concat_axis=0, tiled=True)  13.8 us
    all_gather x1, blocking collectives, shards(): lax.all_gather(row_back, 'tp', axis=2, tiled=True)  13.7 us
  transfers between devices with their start and end apart: 9, of which 8 were waited for; matrix products, arithmetic and copies ran while one was open for 14% of the time, Pallas kernels for 0%

profile of v1, /device:TPU:0, one launch (start us, length us, event | category | flops | bytes accessed | tf_op | source)
XLA Modules:
  0.0 351.3 jit_solution(8533961253590650615)
XLA Ops:
  18.6 18.8 %all-gather.3.cloned.1.call-done = f32[512,768]{1,0:T(8,128)} async-done(((f32[128,768]{1,0:T(8,128)}), f32[512,768]{1,0:T(8,128)}) %all-gather.3.cloned.1.call-update) | async-done | bytes 1572880 | tf_op jit(solution)/shard_map/all_gather | solution.py:15
  40.4 2.7 gather_fusion
  43.1 5.6 %all-to-all-start = ((bf16[8,64,768]{2,1,0:T(8,128)(2,1)}), bf16[8,64,768]{2,1,0:T(8,128)(2,1)}, u32[]{:S(2)}, u32[]{:S(2)}) async-start(bf16[8,64,768]{2,1,0:T(8,128)(2,1)} %bitcast.14), calls=%async_computation | async-start | bytes 1572864 | tf_op jit(solution)/shard_map/all_to_all | solution.py:141
  52.9 2.7 gather_fusion.2
  55.7 13.8 %all-to-all-done = bf16[8,64,768]{2,1,0:T(8,128)(2,1)} async-done(((bf16[8,64,768]{2,1,0:T(8,128)(2,1)}), bf16[8,64,768]{2,1,0:T(8,128)(2,1)}, u32[]{:S(2)}, u32[]{:S(2)}) %all-to-all-start) | async-done | bytes 786464 | tf_op jit(solution)/shard_map/all_to_all | solution.py:141
  69.4 4.3 %all-to-all-start.2 = ((bf16[8,64,768]{2,1,0:T(8,128)(2,1)}), bf16[8,64,768]{2,1,0:T(8,128)(2,1)}, u32[]{:S(2)}, u32[]{:S(2)}) async-start(bf16[8,64,768]{2,1,0:T(8,128)(2,1)} %bitcast.26), calls=%async_computation.2 | async-start | bytes 1572864 | tf_op jit(solution)/shard_map/all_to_all | solution.py:176
  82.8 10.9 %all-to-all-done.2 = bf16[8,64,768]{2,1,0:T(8,128)(2,1)} async-done(((bf16[8,64,768]{2,1,0:T(8,128)(2,1)}), bf16[8,64,768]{2,1,0:T(8,128)(2,1)}, u32[]{:S(2)}, u32[]{:S(2)}) %all-to-all-start.2) | async-done | bytes 786464 | tf_op jit(solution)/shard_map/all_to_all | solution.py:176
  93.7 3.1 fusion.13
  97.8 2.1 fusion.16
  99.9 2.3 copy.98
  102.1 3.7 %reshape.493 = f32[768,512]{1,0:T(8,128)} reshape(f32[768,8,64]{2,1,0:T(8,128)} %bitcast.150) | data formatting | bytes 3145728
  108.5 5.5 %all-to-all-start.1 = ((bf16[8,64,192]{2,1,0:T(8,128)(2,1)}), bf16[8,64,192]{2,1,0:T(8,128)(2,1)S(1)}, u32[]{:S(2)}, u32[]{:S(2)}) async-start(bf16[8,64,192]{2,1,0:T(8,128)(2,1)} %copy.97), calls=%async_computation.1 | async-start | bytes 524288 | tf_op jit(solution)/shard_map/all_to_all | solution.py:151
  114.8 8.1 %all-to-all-done.1 = bf16[8,64,192]{2,1,0:T(8,128)(2,1)S(1)} async-done(((bf16[8,64,192]{2,1,0:T(8,128)(2,1)}), bf16[8,64,192]{2,1,0:T(8,128)(2,1)S(1)}, u32[]{:S(2)}, u32[]{:S(2)}) %all-to-all-start.1) | async-done | bytes 196640 | tf_op jit(solution)/shard_map/all_to_all | solution.py:151
  123.2 20.0 %all_gather.14 = bf16[8,64,768]{1,0,2:T(8,128)(2,1)} all-gather(bf16[8,64,192]{1,0,2:T(8,128)(2,1)S(1)} %copy.81), channel_id=1, replica_groups=mesh['ex'=8,'tp'=4] {'tp'}, dimensions={2}, use_global_device_ids=true | all-gather | bytes 983040 | tf_op jit(solution)/shard_map/all_gather | solution.py:157
  146.8 2.4 multiply_reduce_fusion
  151.5 3.4 all-to-all-start.3
  155.1 9.5 %all-to-all-done.3 = bf16[8,64,192]{2,1,0:T(8,128)(2,1)S(1)} async-done(((bf16[8,64,192]{2,1,0:T(8,128)(2,1)}), bf16[8,64,192]{2,1,0:T(8,128)(2,1)S(1)}, u32[]{:S(2)}, u32[]{:S(2)}) %all-to-all-start.3) | async-done | bytes 196640 | tf_op jit(solution)/shard_map/all_to_all | solution.py:195
  164.8 13.7 %all_gather.15 = bf16[8,64,768]{1,0,2:T(8,128)(2,1)} all-gather(bf16[8,64,192]{1,0,2:T(8,128)(2,1)S(1)} %copy.86), channel_id=1, replica_groups=mesh['ex'=8,'tp'=4] {'tp'}, dimensions={2}, use_global_device_ids=true | all-gather | bytes 983040 | tf_op jit(solution)/shard_map/all_gather | solution.py:196
  195.1 3.5 convolution_bitcast_fusion.1
  198.6 3.5 %convolution_bitcast_fusion = f32[1,768,768]{2,1,0:T(8,128)} fusion(bf16[8,64,768]{2,1,0:T(8,128)(2,1)} %all-to-all-done.2, f32[8,64,768]{2,1,0:T(8,128)S(1)} %copy-done.47), kind=kOutput, calls=%fused_computation.10 | convolution fusion | flops 607518720 | bytes 4718592 | tf_op jit(solution)/shard_map/slcf,slcd->lfd/dot_general | solution.py:183
  203.5 21.0 %all-reduce.7.cloned.1.call-done = bf16[128,768]{1,0:T(8,128)(2,1)} async-done(((bf16[128,768]{1,0:T(8,128)(2,1)}), bf16[128,768]{1,0:T(8,128)(2,1)}) %all-reduce.7.cloned.1.call-update) | async-done | bytes 196624 | tf_op jit(solution)/shard_map/psum | solution.py:251
  225.7 40.1 %all-reduce.2 = (f32[768]{0:T(1024)}, f32[768]{0:T(1024)}, f32[32,3]{0,1:T(4,128)}, f32[768,8]{0,1:T(8,128)}) all-reduce(f32[768]{0:T(1024)S(1)} %get-tuple-element.16, f32[768]{0:T(1024)S(1)} %get-tuple-element.12, f32[32,3]{0,1:T(4,128)S(1)} %fusion.25, f32[768,8]{0,1:T(8,128)S(1)} %fusion.98), channel_id=1, replica_groups=mesh['ex'=8,'tp'=4] {'ex'}, use_global_device_ids=true, to_apply=%region_30.31 | all-reduce | flops 7776 | bytes 62208 | tf_op jit(solution)/shard_map/psum | solution.py:259
  267.6 72.7 %all-reduce.9.cloned.1.call-done = (f32[768,192]{0,1:T(8,128)}, f32[768,192]{0,1:T(8,128)}, f32[768,192]{0,1:T(8,128)}, f32[192,768]{1,0:T(8,128)}) async-done(((f32[768,192]{0,1:T(8,128)}, f32[768,192]{0,1:T(8,128)}, f32[768,192]{0,1:T(8,128)}, f32[192,768]{1,0:T(8,128)}), (f32[768,192]{0,1:T(8,128)}, f32[768,192]{0,1:T(8,128)}, f32[768,192]{0,1:T(8,128)}, ...) | async-done | bytes 2359312 | tf_op jit(solution)/shard_map/psum | solution.py:259
  340.3 2.0 copy.105
  (210 shorter events, 61.1 us)
Async XLA Ops:
  7.2 69.7 %copy-start = (bf16[1,768,768]{2,1,0:T(8,128)(2,1)S(1)}, bf16[1,768,768]{2,1,0:T(8,128)(2,1)}, u32[]{:S(2)}) copy-start(bf16[1,768,768]{2,1,0:T(8,128)(2,1)} %param.26) | copy-start | bytes 3538948
  7.2 4.5 %copy-start.1 = (bf16[128,768]{1,0:T(8,128)(2,1)S(1)}, bf16[128,768]{1,0:T(8,128)(2,1)}, u32[]{:S(2)}) copy-start(bf16[128,768]{1,0:T(8,128)(2,1)} %param.14) | copy-start | bytes 589828
  7.2 4.5 %copy-start.26 = (f32[768]{0:T(1024)S(1)}, f32[768]{0:T(1024)}, u32[]{:S(2)}) copy-start(f32[768]{0:T(1024)} %param.21) | copy-start | bytes 9220
  7.2 4.8 %copy-start.18 = (bf16[768,192]{0,1:T(8,128)(2,1)S(1)}, bf16[768,192]{0,1:T(8,128)(2,1)}, u32[]{:S(2)}) copy-start(bf16[768,192]{0,1:T(8,128)(2,1)} %param.18) | copy-start | bytes 884740
  7.2 5.1 %copy-start.45 = (s32[1,4]{1,0:T(1,128)S(1)}, s32[1,4]{1,0:T(1,128)}, u32[]{:S(2)}) copy-start(s32[1,4]{1,0:T(1,128)} %param.16) | copy-start | bytes 52
  7.3 30.2 %all-gather.3.cloned.1.call-start = ((), (), s32[]{:S(2)}) async-start(), calls=%async_computation.7 | async-start | bytes 1966080 | tf_op jit(solution)/shard_map/all_gather | solution.py:15
  7.4 5.3 %copy-start.27 = (s32[128,128]{1,0:T(8,128)}, s32[128,128]{1,0:T(8,128)S(1)}, u32[]{:S(2)}) copy-start(s32[128,128]{1,0:T(8,128)S(1)} %compare_select_fusion) | copy-start | bytes 196612
  12.4 25.1 %copy-start.22 = (bf16[128,192]{0,1:T(8,128)(2,1)}, bf16[128,192]{0,1:T(8,128)(2,1)S(1)}, u32[]{:S(2)}) copy-start(bf16[128,192]{0,1:T(8,128)(2,1)S(1)} %convolution_convert_fusion.4) | copy-start | bytes 147460
  15.4 24.2 %copy-start.30 = (f32[768]{0:T(1024)S(1)}, f32[768]{0:T(1024)}, u32[]{:S(2)}) copy-start(f32[768]{0:T(1024)} %param.22) | copy-start | bytes 9220
  16.5 20.9 %copy-start.42 = (s32[256,1]{0,1:T(1,128)}, s32[256,1]{0,1:T(1,128)S(1)}, u32[]{:S(2)}) copy-start(s32[256,1]{0,1:T(1,128)S(1)} %compare_select_fusion.1) | copy-start | bytes 3076
  43.1 5.6 %copy-start.4 = (bf16[128,768]{1,0:T(8,128)(2,1)S(1)}, bf16[128,768]{1,0:T(8,128)(2,1)}, u32[]{:S(2)}) copy-start(bf16[128,768]{1,0:T(8,128)(2,1)} %param.27) | copy-start | bytes 589828
  43.1 26.3 %all-to-all-start = ((bf16[8,64,768]{2,1,0:T(8,128)(2,1)}), bf16[8,64,768]{2,1,0:T(8,128)(2,1)}, u32[]{:S(2)}, u32[]{:S(2)}) async-start(bf16[8,64,768]{2,1,0:T(8,128)(2,1)} %bitcast.14), calls=%async_computation | async-start | bytes 1572864 | tf_op jit(solution)/shard_map/all_to_all | solution.py:141
  69.4 24.3 %all-to-all-start.2 = ((bf16[8,64,768]{2,1,0:T(8,128)(2,1)}), bf16[8,64,768]{2,1,0:T(8,128)(2,1)}, u32[]{:S(2)}, u32[]{:S(2)}) async-start(bf16[8,64,768]{2,1,0:T(8,128)(2,1)} %bitcast.26), calls=%async_computation.2 | async-start | bytes 1572864 | tf_op jit(solution)/shard_map/all_to_all | solution.py:176
  73.8 32.6 %reduce-scatter.7.cloned.1.call-start = ((), (), s32[]{:S(2)}) async-start(), calls=%async_computation.8 | async-start | bytes 983040
  82.6 66.7 %reduce-scatter.9.cloned.1.call-start = ((), (), s32[]{:S(2)}) async-start(), calls=%async_computation.9 | async-start | bytes 1966080
  105.9 8.1 %copy-start.5 = (bf16[128,768]{1,0:T(8,128)(2,1)S(1)}, bf16[128,768]{1,0:T(8,128)(2,1)}, u32[]{:S(2)}) copy-start(bf16[128,768]{1,0:T(8,128)(2,1)} %param.27) | copy-start | bytes 589828
  105.9 8.9 %copy-start.43 = (s32[256,1]{0,1:T(1,128)S(1)}, s32[256,1]{0,1:T(1,128)}, u32[]{:S(2)}) copy-start(s32[256,1]{0,1:T(1,128)} %copy-done.42) | copy-start | bytes 3076
  108.5 14.4 %all-to-all-start.1 = ((bf16[8,64,192]{2,1,0:T(8,128)(2,1)}), bf16[8,64,192]{2,1,0:T(8,128)(2,1)S(1)}, u32[]{:S(2)}, u32[]{:S(2)}) async-start(bf16[8,64,192]{2,1,0:T(8,128)(2,1)} %copy.97), calls=%async_computation.1 | async-start | bytes 524288 | tf_op jit(solution)/shard_map/all_to_all | solution.py:151
  146.8 8.2 %copy-start.34 = (f32[128]{0:T(128)S(1)}, f32[128]{0:T(128)}, u32[]{:S(2)}) copy-start(f32[128]{0:T(128)} %copy-done.33) | copy-start | bytes 1540
  146.8 8.2 %copy-start.39 = (f32[128]{0:T(128)S(1)}, f32[128]{0:T(128)}, u32[]{:S(2)}) copy-start(f32[128]{0:T(128)} %copy-done.38) | copy-start | bytes 1540
  146.8 8.2 %copy-start.32 = (s32[128,2]{0,1:T(2,128)S(1)}, s32[128,2]{0,1:T(2,128)}, u32[]{:S(2)}) copy-start(s32[128,2]{0,1:T(2,128)} %param.15) | copy-start | bytes 3076
  151.5 13.1 %all-to-all-start.3 = ((bf16[8,64,192]{2,1,0:T(8,128)(2,1)}), bf16[8,64,192]{2,1,0:T(8,128)(2,1)S(1)}, u32[]{:S(2)}, u32[]{:S(2)}) async-start(bf16[8,64,192]{2,1,0:T(8,128)(2,1)} %copy.99), calls=%async_computation.3 | async-start | bytes 524288 | tf_op jit(solution)/shard_map/all_to_all | solution.py:195
  154.9 69.6 %all-reduce.7.cloned.1.call-start = ((), (), s32[]{:S(2)}) async-start(), calls=%async_computation.6 | async-start | bytes 393216 | tf_op jit(solution)/shard_map/psum | solution.py:251
  193.9 146.4 %all-reduce.9.cloned.1.call-start = ((), (), s32[]{:S(2)}) async-start(), calls=%async_computation.10 | async-start | bytes 4718592 | tf_op jit(solution)/shard_map/psum | solution.py:259
  (35 other events, 84.0 us)
Sparse Core Ops, SparseCore 0:
  15.0 22.3 all-gather.2
  82.7 23.6 reduce-scatter.6
  109.7 33.9 reduce-scatter.8
  194.0 30.4 all-reduce.6
  229.4 110.8 all-reduce.8
